TPU v7x, 128 devices: a whole 4x4x4 slice. The times are simulated.
128 devices in a mesh: rows: 32 (over z, x, core), half: 4 (over y).
Axes of the slice: x: 4, y: 4, z: 4, core: 2. Of those that a mesh axis runs over, the one named last changes fastest.
Arguments:
- pair: bfloat16 [1024, 1024, 128], P('rows', 'half'), may hold values from -6 to 6
- pair_mask: int32 [1024, 1024], P('rows', 'half'), may hold values from 0 to 1, as said below
- gains: float32 [3, 128], replicated, may hold values from 0.1 to 1.9
- w_tri: bfloat16 [128, 640], replicated, may hold values from -0.5 to 0.5
- w_tri_out: bfloat16 [128, 128], replicated, may hold values from -0.5 to 0.5
- w_att: bfloat16 [128, 512], replicated, may hold values from -0.5 to 0.5
- w_bias: bfloat16 [128, 4], replicated, may hold values from -0.5 to 0.5
- w_att_out: bfloat16 [128, 128], replicated, may hold values from -0.5 to 0.5
Outputs:
- updated: bfloat16 [1024, 1024, 128], P('rows', 'half')
Inputs may be any that keep to these rules, and one draw needn't show every extreme that they name: The last tokens of the crop are padding, between 102 and 2 * (102) of them: pair_mask[i, k] is 0 wherever token i or token k is padding. Other pairs may be 0 as well.
All inputs are finite; a program needn't handle non-finite values.
Results may differ from a plain program's by a relative error of at most 0.012.
Values may be sent and summed in bfloat16 or wider, within the bound.
No kernel may reach another device: no remote copies, remote signals or barrier semaphores. Data moves between devices by JAX's collectives and lax.ppermute only.
A program may use at most 128 MiB of HBM per device.

v0:
```python
import math
import jax
import jax.numpy as jnp
from jax import lax
from jax.sharding import PartitionSpec as P


def layer_norm(value, gain, axis):
    center = value - jnp.mean(value, axis=axis, keepdims=True)
    spread = jnp.mean(center * center, axis=axis, keepdims=True)
    return center * lax.rsqrt(spread + 1e-05) * gain


def shards(pair, pair_mask, gains, w_tri, w_tri_out, w_att, w_bias, w_att_out):
    rows_here, cols_here, width = pair.shape
    field = pair.astype(jnp.float32)
    normed = layer_norm(field, gains[0], -1).astype(jnp.bfloat16)
    edges = jnp.einsum(
        "ikc,cd->dik", normed, w_tri[:, : 4 * width], preferred_element_type=jnp.float32
    )
    weight_mask = pair_mask.astype(jnp.float32)
    left_edge = (weight_mask * jax.nn.sigmoid(edges[width : 2 * width]) * edges[:width]).astype(
        jnp.bfloat16
    )
    right_edge = (
        weight_mask * jax.nn.sigmoid(edges[3 * width :]) * edges[2 * width : 3 * width]
    ).astype(jnp.bfloat16)
    gate_field = jax.nn.sigmoid(
        jnp.einsum("ikc,cd->ikd", normed, w_tri[:, 4 * width :], preferred_element_type=jnp.float32)
    )
    left_all, right_all = (
        lax.all_to_all(left_edge, "rows", split_axis=0, concat_axis=1, tiled=True),
        lax.all_to_all(right_edge, "rows", split_axis=0, concat_axis=1, tiled=True),
    )
    product = lax.psum_scatter(
        jnp.einsum("cik,cjk->jci", left_all, right_all, preferred_element_type=jnp.float32).astype(
            jnp.bfloat16
        ),
        "half",
        scatter_dimension=0,
        tiled=True,
    )
    returned = lax.all_to_all(product, "rows", split_axis=2, concat_axis=1, tiled=True)
    tri_normed = layer_norm(returned.astype(jnp.float32), gains[1][:, None], 1).astype(jnp.bfloat16)
    update = jnp.einsum("jci,cd->ijd", tri_normed, w_tri_out, preferred_element_type=jnp.float32)
    after_mult = (field + gate_field * update).astype(jnp.bfloat16)
    att_normed = layer_norm(after_mult.astype(jnp.float32), gains[2], -1).astype(jnp.bfloat16)
    projected = jnp.einsum(
        "ijc,cd->ijd", att_normed, w_att, preferred_element_type=jnp.float32
    ).astype(jnp.bfloat16)
    queries = projected[..., :width]
    keys_here = projected[..., width : 2 * width]
    values_here = projected[..., 2 * width : 3 * width]
    gate_attn = projected[..., 3 * width :]
    bias_local = jnp.einsum(
        "ijc,ch->hij", att_normed, w_bias, preferred_element_type=jnp.float32
    ).astype(jnp.bfloat16)
    bias_rows = lax.all_gather(bias_local, "rows", axis=1, tiled=True)
    bias_full = lax.all_gather(bias_rows, "half", axis=2, tiled=True)
    bias_mine = lax.dynamic_slice_in_dim(
        bias_full, lax.axis_index("half") * cols_here, cols_here, 1
    )
    heads = w_bias.shape[1]
    head_dim = width // heads
    scale = head_dim ** (-0.5)
    group = math.gcd(rows_here, 4)
    blocks = rows_here // group
    query_groups = queries.reshape(blocks, group, cols_here, heads, head_dim)
    mask_wire = pair_mask.astype(jnp.bfloat16)
    piece_keys = lax.all_gather(keys_here, "half", axis=1, tiled=True)
    piece_values = lax.all_gather(values_here, "half", axis=1, tiled=True)
    piece_mask = lax.all_gather(mask_wire, "half", axis=1, tiled=True)
    span = piece_keys.shape[1]
    bias_piece = bias_mine.astype(jnp.float32)
    key_groups = piece_keys.reshape(blocks, group, span, heads, head_dim)
    value_groups = piece_values.reshape(blocks, group, span, heads, head_dim)
    mask_groups = piece_mask.astype(jnp.float32).reshape(blocks, group, span)

    def one_block(items):
        query_block, key_block, value_block, mask_block, running, peak, denom = items
        scores = (
            jnp.einsum(
                "gjhd,gkhd->ghjk", query_block, key_block, preferred_element_type=jnp.float32
            )
            * scale
        )
        scores = scores + bias_piece[None]
        scores = jnp.where(mask_block[:, None, None, :] > 0.5, scores, -1000000000.0)
        new_peak = jnp.maximum(peak, jnp.max(scores, axis=-1))
        shrink = jnp.exp(peak - new_peak)
        weights = jnp.exp(scores - new_peak[..., None])
        denom = denom * shrink + jnp.sum(weights, axis=-1)
        running = running * shrink[..., None] + jnp.einsum(
            "ghjk,gkhd->ghjd",
            weights.astype(jnp.bfloat16),
            value_block,
            preferred_element_type=jnp.float32,
        )
        return (running, new_peak, denom)

    running = jnp.zeros((blocks, group, heads, cols_here, head_dim), jnp.float32)
    peak = jnp.full((blocks, group, heads, cols_here), -1e30, jnp.float32)
    denom = jnp.zeros((blocks, group, heads, cols_here), jnp.float32)
    running, peak, denom = lax.map(
        one_block, (query_groups, key_groups, value_groups, mask_groups, running, peak, denom)
    )
    attended = (running / denom[..., None]).reshape(rows_here, heads, cols_here, head_dim)
    attended = jnp.transpose(attended, (0, 2, 1, 3)).reshape(rows_here, cols_here, width)
    gated = (attended * jax.nn.sigmoid(gate_attn.astype(jnp.float32))).astype(jnp.bfloat16)
    output = jnp.einsum("ijc,cd->ijd", gated, w_att_out, preferred_element_type=jnp.float32)
    return (after_mult.astype(jnp.float32) + output).astype(jnp.bfloat16)


def solution(mesh):
    in_specs = (P("rows", "half", None), P("rows", "half"), P(), P(), P(), P(), P(), P())
    out_specs = P("rows", "half", None)
    return jax.shard_map(shards, mesh=mesh, in_specs=in_specs, out_specs=out_specs, check_vma=False)
```

profile of v0, /device:TPU:0, one launch (start us, length us, event | category | flops | bytes accessed | tf_op | source)
XLA Modules:
  0.0 692.3 jit_solution(11790933083862708372)
XLA Ops:
  21.9 8.4 %all-to-all-start = ((bf16[128,32,256]{2,1,0:T(8,128)(2,1)}), bf16[128,32,256]{2,1,0:T(8,128)(2,1)}, u32[]{:S(2)}, u32[]{:S(2)}) async-start(bf16[128,32,256]{2,1,0:T(8,128)(2,1)} %copy.48), calls=%async_computation | async-start | bytes 4194304 | tf_op jit(solution)/shard_map/all_to_all | solution.py:33
  34.9 25.3 %all-to-all-done = bf16[128,32,256]{2,1,0:T(8,128)(2,1)} async-done(((bf16[128,32,256]{2,1,0:T(8,128)(2,1)}), bf16[128,32,256]{2,1,0:T(8,128)(2,1)}, u32[]{:S(2)}, u32[]{:S(2)}) %all-to-all-start) | async-done | bytes 2097184 | tf_op jit(solution)/shard_map/all_to_all | solution.py:33
  68.2 26.8 %all-to-all-done.1 = bf16[128,32,256]{2,1,0:T(8,128)(2,1)} async-done(((bf16[128,32,256]{2,1,0:T(8,128)(2,1)}), bf16[128,32,256]{2,1,0:T(8,128)(2,1)}, u32[]{:S(2)}, u32[]{:S(2)}) %all-to-all-start.1) | async-done | bytes 2097184 | tf_op jit(solution)/shard_map/all_to_all | solution.py:32
  97.1 5.6 convert_bitcast_fusion
  102.8 77.8 %reduce-scatter.2.cloned.1.call-done = bf16[256,4,1024]{2,0,1:T(8,128)(2,1)} async-done(((bf16[1024,4,1024]{2,0,1:T(8,128)(2,1)}), bf16[256,4,1024]{2,0,1:T(8,128)(2,1)}) %reduce-scatter.2.cloned.1.call-update) | async-done | bytes 2097168 | tf_op jit(solution)/shard_map/reduce_scatter | solution.py:35
  184.8 35.8 %all_to_all.45 = bf16[256,4,1024]{0,1,2:T(4,128)(2,1)S(1)} all-to-all(bf16[256,4,1024]{0,1,2:T(4,128)(2,1)} %copy.52), channel_id=1, replica_groups=mesh['rows'=32,'half'=4] {'rows'}, dimensions={2} | all-to-all | bytes 4194304 | tf_op jit(solution)/shard_map/all_to_all | solution.py:43
  230.1 40.1 %all-gather.7.cloned.1.call-done = bf16[4,1024,256]{2,0,1:T(4,128)(2,1)} async-done(((bf16[4,32,256]{2,0,1:T(4,128)(2,1)}), bf16[4,1024,256]{2,0,1:T(4,128)(2,1)}) %all-gather.7.cloned.1.call-update) | async-done | bytes 2097168 | tf_op jit(solution)/shard_map/all_gather | solution.py:58
  279.5 12.6 %all_gather.15 = bf16[32,1024]{1,0:T(8,128)(2,1)S(1)} all-gather(bf16[32,256]{1,0:T(8,128)(2,1)S(1)} %get-tuple-element.101), channel_id=1, replica_groups=mesh['rows'=32,'half'=4] {'half'}, dimensions={1}, use_global_device_ids=true | all-gather | bytes 81920 | tf_op jit(solution)/shard_map/all_gather | solution.py:72
  292.1 67.1 %all-gather.9.cloned.1.call-done = bf16[4,1024,1024]{2,0,1:T(4,128)(2,1)} async-done(((bf16[4,1024,256]{2,0,1:T(4,128)(2,1)}), bf16[4,1024,1024]{2,0,1:T(4,128)(2,1)}) %all-gather.9.cloned.1.call-update) | async-done | bytes 8388624 | tf_op jit(solution)/shard_map/all_gather | solution.py:59
  366.4 81.8 %all-gather.5.cloned.1.call-done = bf16[32,1024,128]{1,2,0:T(8,128)(2,1)} async-done(((bf16[32,256,128]{1,2,0:T(8,128)(2,1)}), bf16[32,1024,128]{1,2,0:T(8,128)(2,1)}) %all-gather.5.cloned.1.call-update) | async-done | bytes 8388624 | tf_op jit(solution)/shard_map/all_gather | solution.py:70
  448.2 89.3 %all-gather.11.cloned.1.call-done = bf16[32,1024,128]{1,2,0:T(8,128)(2,1)} async-done(((bf16[32,256,128]{1,2,0:T(8,128)(2,1)}), bf16[32,1024,128]{1,2,0:T(8,128)(2,1)}) %all-gather.11.cloned.1.call-update) | async-done | bytes 8388624 | tf_op jit(solution)/shard_map/all_gather | solution.py:71
  537.5 138.9 %while.12 = (s32[]{:T(128)}, f32[8,4,4,256,32]{3,4,2,1,0:T(8,128)}, f32[8,4,4,256]{3,2,1,0:T(4,128)S(1)}, f32[8,4,1024]{2,1,0:T(4,128)S(1)}, bf16[8,4,256,4,32]{...) while((s32[]{:T(128)}, f32[8,4,4,256,32]{3,4,2,1,0:T(8,128)}, ...), condition=%wide.region_10.11_spmd, body=%wide.region_7.10_spmd.sunk | while | flops 595746816 | bytes 82790528 | solution.py:104
  537.6 5.8 fusion.83
  543.4 5.0 fusion.85
  548.4 6.6 fusion.84
  555.1 5.6 fusion.83
  560.8 5.0 fusion.85
  565.8 6.6 fusion.84
  572.4 5.7 fusion.83
  578.2 5.0 fusion.85
  583.2 6.6 fusion.84
  589.9 5.5 fusion.83
  600.4 6.6 fusion.84
  607.1 5.5 fusion.83
  617.7 6.6 fusion.84
  624.3 5.7 fusion.83
  635.1 6.6 fusion.84
  641.7 5.6 fusion.83
  647.4 5.0 fusion.85
  652.4 6.7 fusion.84
  659.1 5.6 fusion.83
  669.8 6.7 fusion.84
  (116 shorter events, 89.9 us)
Async XLA Ops:
  6.5 263.8 %copy-start = (bf16[128,512]{1,0:T(8,128)(2,1)S(1)}, bf16[128,512]{1,0:T(8,128)(2,1)}, u32[]{:S(2)}) copy-start(bf16[128,512]{1,0:T(8,128)(2,1)} %param.15) | copy-start | bytes 393220
  6.5 4.4 copy-start.10
  6.5 4.4 copy-start.9
  6.5 4.5 copy-start.7
  21.9 38.3 %all-to-all-start = ((bf16[128,32,256]{2,1,0:T(8,128)(2,1)}), bf16[128,32,256]{2,1,0:T(8,128)(2,1)}, u32[]{:S(2)}, u32[]{:S(2)}) async-start(bf16[128,32,256]{2,1,0:T(8,128)(2,1)} %copy.48), calls=%async_computation | async-start | bytes 4194304 | tf_op jit(solution)/shard_map/all_to_all | solution.py:33
  60.2 34.7 %all-to-all-start.1 = ((bf16[128,32,256]{2,1,0:T(8,128)(2,1)}), bf16[128,32,256]{2,1,0:T(8,128)(2,1)}, u32[]{:S(2)}, u32[]{:S(2)}) async-start(bf16[128,32,256]{2,1,0:T(8,128)(2,1)} %copy.50), calls=%async_computation.1 | async-start | bytes 4194304 | tf_op jit(solution)/shard_map/all_to_all | solution.py:32
  65.0 115.6 %reduce-scatter.2.cloned.1.call-start = ((), (), s32[]{:S(2)}) async-start(), calls=%async_computation.4 | async-start | bytes 10485760 | tf_op jit(solution)/shard_map/reduce_scatter | solution.py:35
  94.9 2.2 copy-start.4
  102.8 167.5 %all-gather.7.cloned.1.call-start = ((), (), s32[]{:S(2)}) async-start(), calls=%async_computation.6 | async-start | bytes 2162688 | tf_op jit(solution)/shard_map/all_gather | solution.py:58
  222.7 0.8 copy-start.8
  225.2 3.5 copy-start.12
  227.3 1.3 copy-start.5
  230.1 129.1 %all-gather.9.cloned.1.call-start = ((), (), s32[]{:S(2)}) async-start(), calls=%async_computation.7 | async-start | bytes 10485760 | tf_op jit(solution)/shard_map/all_gather | solution.py:59
  270.3 178.0 %all-gather.5.cloned.1.call-start = ((), (), s32[]{:S(2)}) async-start(), calls=%async_computation.5 | async-start | bytes 10485760 | tf_op jit(solution)/shard_map/all_gather | solution.py:70
  274.4 4.5 copy-start.3
  278.9 258.7 %all-gather.11.cloned.1.call-start = ((), (), s32[]{:S(2)}) async-start(), calls=%async_computation.8 | async-start | bytes 10485760 | tf_op jit(solution)/shard_map/all_gather | solution.py:71
  537.6 5.9 copy-start.2
  555.1 5.7 copy-start.2
  572.4 5.8 copy-start.2
  589.9 5.6 copy-start.2
  607.1 5.6 copy-start.2
  624.3 5.8 copy-start.2
  641.7 5.7 copy-start.2
  659.1 5.6 copy-start.2
  676.4 3.2 copy-start.6
  676.4 3.3 copy-start.11
  679.7 6.1 copy-start.1
Sparse Core Ops, SparseCore 0:
  102.9 77.6 reduce-scatter.1
  230.2 40.0 all-gather.6
  271.9 87.2 all-gather.8
  360.7 87.4 all-gather.4
  449.7 87.7 all-gather.10
where the time goes:
time: 693 us; the launch traced here: 692 us
  waiting for transfers between devices  409 us (59%)
  matrix products  119 us (17%)
  other arithmetic  54.1 us (8%)
  blocking collectives  48.4 us (7%)
  local copies, waits for them, and re-layouts  35.1 us (5%)
  between operations  13.4 us (2%)
  starting transfers between devices  13.3 us (2%)
    all_gather x1, waiting for transfers between devices, shards(): piece_values = lax.all_gather(values_here, 'half', axis=1, tiled=True)  89.3 us
    all_gather x1, waiting for transfers between devices, shards(): piece_keys = lax.all_gather(keys_here, 'half', axis=1, tiled=True)  81.8 us
    reduce_scatter x1, waiting for transfers between devices, shards(): lax.psum_scatter(jnp.einsum('cik,cjk->jci', left_all, right_all, preferre...  77.8 us
    all_gather x1, waiting for transfers between devices, shards(): bias_full = lax.all_gather(bias_rows, 'half', axis=2, tiled=True)  67.1 us
    dot_general x8, matrix products, one_block(): jnp.einsum('ghjk,gkhd->ghjd', weights.astype(jnp.bfloat16), value_block,...  53.1 us
    dot_general x8, matrix products, one_block(): jnp.einsum('gjhd,gkhd->ghjk', query_block, key_block, preferred_element_t...  45.2 us
    all_gather x1, waiting for transfers between devices, shards(): bias_rows = lax.all_gather(bias_local, 'rows', axis=1, tiled=True)  40.1 us
    reduce_sum x8, other arithmetic, one_block(): denom = denom * shrink + jnp.sum(weights, axis=-1)  39.8 us
  transfers between devices with their start and end apart: 7, of which 7 were waited for; matrix products, arithmetic and copies ran while one was open for 3% of the time, Pallas kernels for 0%

commit v1 on v0

--- a/solution.py
+++ b/solution.py
@@ -55,7 +55,9 @@
     bias_local = jnp.einsum(
         "ijc,ch->hij", att_normed, w_bias, preferred_element_type=jnp.float32
     ).astype(jnp.bfloat16)
-    bias_rows = lax.all_gather(bias_local, "rows", axis=1, tiled=True)
+    bias_rows = jnp.concatenate(
+        lax.all_to_all(jnp.stack([bias_local] * lax.axis_size("rows")), "rows", 0, 0), axis=1
+    )
     bias_full = lax.all_gather(bias_rows, "half", axis=2, tiled=True)
     bias_mine = lax.dynamic_slice_in_dim(
         bias_full, lax.axis_index("half") * cols_here, cols_here, 1

time: 693 us -> 686 us (0.990)
  waiting for transfers between devices: 409 us -> 367 us
  blocking collectives: 48.4 us -> 80 us
    all_gather x1 -> x0, waiting for transfers between devices: 40.1 us -> none  [shards(): bias_rows = lax.all_gather(bias_local, 'rows', axis=1, tiled=True)]
    all_to_all x0 -> x1, blocking collectives: none -> 31.9 us  [shards(): lax.all_to_all(jnp.stack([bias_local] * lax.axis_size('rows')), 'rows', 0...]
  transfers between devices with their start and end apart: 7 -> 6, of which waited for: 7 -> 6; matrix products, arithmetic and copies ran while one was open for 3% -> 3% of each run, Pallas kernels for 0% -> 0%
where the time goes in v1:
time: 686 us; the launch traced here: 685 us
  waiting for transfers between devices  367 us (53%)
  matrix products  121 us (18%)
  blocking collectives  80 us (12%)
  other arithmetic  55.2 us (8%)
  local copies, waits for them, and re-layouts  35.5 us (5%)
  between operations  13.4 us (2%)
  starting transfers between devices  13.3 us (2%)
    all_gather x1, waiting for transfers between devices, shards(): piece_values = lax.all_gather(values_here, 'half', axis=1, tiled=True)  89.3 us
    all_gather x1, waiting for transfers between devices, shards(): piece_keys = lax.all_gather(keys_here, 'half', axis=1, tiled=True)  85.3 us
    reduce_scatter x1, waiting for transfers between devices, shards(): lax.psum_scatter(jnp.einsum('cik,cjk->jci', left_all, right_all, preferre...  77.8 us
    all_gather x1, waiting for transfers between devices, shards(): bias_full = lax.all_gather(bias_rows, 'half', axis=2, tiled=True)  61.8 us
    dot_general x8, matrix products, one_block(): jnp.einsum('ghjk,gkhd->ghjd', weights.astype(jnp.bfloat16), value_block,...  53 us
    dot_general x8, matrix products, one_block(): jnp.einsum('gjhd,gkhd->ghjk', query_block, key_block, preferred_element_t...  47.9 us
    reduce_sum x8, other arithmetic, one_block(): denom = denom * shrink + jnp.sum(weights, axis=-1)  39.8 us
    all_to_all x1, blocking collectives, shards(): lax.all_to_all(product, 'rows', split_axis=2, concat_axis=1, tiled=True)  35.8 us
  transfers between devices with their start and end apart: 6, of which 6 were waited for; matrix products, arithmetic and copies ran while one was open for 3% of the time, Pallas kernels for 0%

profile of v1, /device:TPU:0, one launch (start us, length us, event | category | flops | bytes accessed | tf_op | source)
XLA Modules:
  0.0 685.3 jit_solution(9243901974992180033)
XLA Ops:
  21.8 8.4 %all-to-all-start = ((bf16[128,32,256]{2,1,0:T(8,128)(2,1)}), bf16[128,32,256]{2,1,0:T(8,128)(2,1)}, u32[]{:S(2)}, u32[]{:S(2)}) async-start(bf16[128,32,256]{2,1,0:T(8,128)(2,1)} %copy.68), calls=%async_computation | async-start | bytes 4194304 | tf_op jit(solution)/shard_map/all_to_all | solution.py:33
  34.8 25.3 %all-to-all-done = bf16[128,32,256]{2,1,0:T(8,128)(2,1)} async-done(((bf16[128,32,256]{2,1,0:T(8,128)(2,1)}), bf16[128,32,256]{2,1,0:T(8,128)(2,1)}, u32[]{:S(2)}, u32[]{:S(2)}) %all-to-all-start) | async-done | bytes 2097184 | tf_op jit(solution)/shard_map/all_to_all | solution.py:33
  68.1 26.8 %all-to-all-done.1 = bf16[128,32,256]{2,1,0:T(8,128)(2,1)} async-done(((bf16[128,32,256]{2,1,0:T(8,128)(2,1)}), bf16[128,32,256]{2,1,0:T(8,128)(2,1)}, u32[]{:S(2)}, u32[]{:S(2)}) %all-to-all-start.1) | async-done | bytes 2097184 | tf_op jit(solution)/shard_map/all_to_all | solution.py:32
  97.1 5.6 convert_bitcast_fusion
  102.8 77.8 %reduce-scatter.2.cloned.1.call-done = bf16[256,4,1024]{2,0,1:T(8,128)(2,1)} async-done(((bf16[1024,4,1024]{2,0,1:T(8,128)(2,1)}), bf16[256,4,1024]{2,0,1:T(8,128)(2,1)}) %reduce-scatter.2.cloned.1.call-update) | async-done | bytes 2097168 | tf_op jit(solution)/shard_map/reduce_scatter | solution.py:35
  184.8 35.8 %all_to_all.50 = bf16[256,4,1024]{0,1,2:T(4,128)(2,1)S(1)} all-to-all(bf16[256,4,1024]{0,1,2:T(4,128)(2,1)} %copy.72), channel_id=1, replica_groups=mesh['rows'=32,'half'=4] {'rows'}, dimensions={2} | all-to-all | bytes 4194304 | tf_op jit(solution)/shard_map/all_to_all | solution.py:43
  229.1 31.9 %all_to_all.51 = bf16[32,4,32,256]{3,2,1,0:T(8,128)(2,1)S(1)} all-to-all(bf16[32,4,32,256]{3,2,1,0:T(8,128)(2,1)S(1)} %stack.2), channel_id=1, replica_groups=mesh['rows'=32,'half'=4] {'rows'}, dimensions={0} | all-to-all | bytes 4194304 | tf_op jit(solution)/shard_map/all_to_all | solution.py:59
  272.6 12.3 %all_gather.12 = bf16[32,1024]{1,0:T(8,128)(2,1)S(1)} all-gather(bf16[32,256]{1,0:T(8,128)(2,1)S(1)} %get-tuple-element.77), channel_id=1, replica_groups=mesh['rows'=32,'half'=4] {'half'}, dimensions={1}, use_global_device_ids=true | all-gather | bytes 81920 | tf_op jit(solution)/shard_map/all_gather | solution.py:74
  284.9 61.8 %all-gather.6.cloned.1.call-done = bf16[4,1024,1024]{2,1,0:T(8,128)(2,1)} async-done(((bf16[4,1024,256]{2,1,0:T(8,128)(2,1)}), bf16[4,1024,1024]{2,1,0:T(8,128)(2,1)}) %all-gather.6.cloned.1.call-update) | async-done | bytes 8388624 | tf_op jit(solution)/shard_map/all_gather | solution.py:61
  350.9 85.3 %all-gather.4.cloned.1.call-done = bf16[32,1024,128]{1,2,0:T(8,128)(2,1)} async-done(((bf16[32,256,128]{1,2,0:T(8,128)(2,1)}), bf16[32,1024,128]{1,2,0:T(8,128)(2,1)}) %all-gather.4.cloned.1.call-update) | async-done | bytes 8388624 | tf_op jit(solution)/shard_map/all_gather | solution.py:72
  436.1 89.3 %all-gather.8.cloned.1.call-done = bf16[32,1024,128]{1,2,0:T(8,128)(2,1)} async-done(((bf16[32,256,128]{1,2,0:T(8,128)(2,1)}), bf16[32,1024,128]{1,2,0:T(8,128)(2,1)}) %all-gather.8.cloned.1.call-update) | async-done | bytes 8388624 | tf_op jit(solution)/shard_map/all_gather | solution.py:73
  525.5 141.5 %while.12 = (s32[]{:T(128)}, f32[8,4,4,256,32]{3,4,2,1,0:T(8,128)}, f32[8,4,4,256]{3,2,1,0:T(4,128)S(1)}, f32[8,4,1024]{2,1,0:T(4,128)S(1)}, bf16[8,4,256,4,32]{...) while((s32[]{:T(128)}, f32[8,4,4,256,32]{3,4,2,1,0:T(8,128)}, ...), condition=%wide.region_10.11_spmd, body=%wide.region_7.10_spmd.sunk | while | flops 595746816 | bytes 82790528 | solution.py:106
  525.5 6.0 fusion.83
  531.5 5.0 fusion.85
  536.5 6.6 fusion.84
  543.2 6.0 fusion.83
  549.2 5.0 fusion.85
  554.2 6.6 fusion.84
  560.8 6.0 fusion.83
  566.9 5.0 fusion.85
  571.9 6.6 fusion.84
  578.5 6.0 fusion.83
  589.6 6.6 fusion.84
  596.2 6.0 fusion.83
  607.3 6.6 fusion.84
  613.9 6.0 fusion.83
  625.0 6.6 fusion.84
  631.6 6.0 fusion.83
  642.7 6.6 fusion.84
  649.3 6.0 fusion.83
  655.4 5.0 fusion.85
  660.4 6.6 fusion.84
  (116 shorter events, 90.5 us)
Async XLA Ops:
  6.5 256.0 %copy-start = (bf16[128,512]{1,0:T(8,128)(2,1)S(1)}, bf16[128,512]{1,0:T(8,128)(2,1)}, u32[]{:S(2)}) copy-start(bf16[128,512]{1,0:T(8,128)(2,1)} %param.15) | copy-start | bytes 393220
  6.5 4.4 copy-start.10
  6.5 4.4 copy-start.9
  6.5 4.5 copy-start.7
  21.8 38.3 %all-to-all-start = ((bf16[128,32,256]{2,1,0:T(8,128)(2,1)}), bf16[128,32,256]{2,1,0:T(8,128)(2,1)}, u32[]{:S(2)}, u32[]{:S(2)}) async-start(bf16[128,32,256]{2,1,0:T(8,128)(2,1)} %copy.68), calls=%async_computation | async-start | bytes 4194304 | tf_op jit(solution)/shard_map/all_to_all | solution.py:33
  60.2 34.7 %all-to-all-start.1 = ((bf16[128,32,256]{2,1,0:T(8,128)(2,1)}), bf16[128,32,256]{2,1,0:T(8,128)(2,1)}, u32[]{:S(2)}, u32[]{:S(2)}) async-start(bf16[128,32,256]{2,1,0:T(8,128)(2,1)} %copy.70), calls=%async_computation.1 | async-start | bytes 4194304 | tf_op jit(solution)/shard_map/all_to_all | solution.py:32
  64.9 115.6 %reduce-scatter.2.cloned.1.call-start = ((), (), s32[]{:S(2)}) async-start(), calls=%async_computation.5 | async-start | bytes 10485760 | tf_op jit(solution)/shard_map/reduce_scatter | solution.py:35
  94.9 2.2 copy-start.4
  102.7 244.0 %all-gather.6.cloned.1.call-start = ((), (), s32[]{:S(2)}) async-start(), calls=%async_computation.7 | async-start | bytes 10485760 | tf_op jit(solution)/shard_map/all_gather | solution.py:61
  222.6 0.8 copy-start.8
  225.1 2.9 copy-start.12
  227.3 1.8 copy-start.5
  261.0 2.3 copy-start.6
  262.5 173.6 %all-gather.4.cloned.1.call-start = ((), (), s32[]{:S(2)}) async-start(), calls=%async_computation.6 | async-start | bytes 10485760 | tf_op jit(solution)/shard_map/all_gather | solution.py:72
  265.8 6.2 copy-start.3
  272.0 253.5 %all-gather.8.cloned.1.call-start = ((), (), s32[]{:S(2)}) async-start(), calls=%async_computation.8 | async-start | bytes 10485760 | tf_op jit(solution)/shard_map/all_gather | solution.py:73
  525.5 6.0 copy-start.2
  543.1 6.0 copy-start.2
  560.8 6.0 copy-start.2
  578.5 6.0 copy-start.2
  596.2 6.0 copy-start.2
  613.9 6.0 copy-start.2
  631.6 6.0 copy-start.2
  649.3 6.0 copy-start.2
  667.0 3.1 copy-start.11
  670.1 8.7 %copy-start.1 = (bf16[128,512]{1,0:T(8,128)(2,1)S(1)}, bf16[128,512]{1,0:T(8,128)(2,1)}, u32[]{:S(2)}) copy-start(bf16[128,512]{1,0:T(8,128)(2,1)} %param.15) | copy-start | bytes 393220
Sparse Core Ops, SparseCore 0:
  102.9 77.6 reduce-scatter.1
  262.6 84.0 all-gather.5
  348.4 87.6 all-gather.3
  437.6 87.7 all-gather.7
